TPU v7x, 512 devices: a whole 4x4x16 slice. The times are simulated.
512 devices in a mesh: ctx: 128 (over x_lo, y, z), ch: 4 (over x_hi, core).
Axes of the slice: x: 4 (x_hi: 2, x_lo: 2; x = x_hi * 2 + x_lo), y: 4, z: 16, core: 2. Of those that a mesh axis runs over, the one named last changes fastest.
Arguments:
- query_in: bfloat16 [16384, 4096], P('ctx', 'ch'), may hold values from -6 to 6
- key_in: bfloat16 [16384, 4096], P('ctx', 'ch'), may hold values from -6 to 6
- value_in: bfloat16 [16384, 4096], P('ctx', 'ch'), may hold values from -6 to 6
- short_filter: float32 [3, 3, 4096], P(None, None, 'ch'), may hold values from -3.5 to 3.5
- decay_rate: float32 [4096, 16], P('ch'), may hold values from 0.5 to 2000
- residue: float32 [4096, 16], P('ch'), may hold values from -1.5 to 1.5
- out_weight: bfloat16 [4096, 4096], P('ch', 'ctx'), may hold values from -0.09375 to 0.09375
Outputs:
- mixed: bfloat16 [16384, 4096], P(('ctx', 'ch'))
All inputs are finite; a program needn't handle non-finite values.
Results may differ from a plain program's by a relative error of at most 0.0081.
Values may be sent and summed in bfloat16 or wider, within the bound.
A program may use at most 128 MiB of HBM per device.

v0:
```python
import math

import jax
import jax.numpy as jnp
from jax import lax
from jax.sharding import PartitionSpec as P

SHORT_TAPS = 3


HIGHEST = lax.Precision.HIGHEST


def from_behind(block, axis, distance):
    devices = range(lax.axis_size(axis))
    route = [(i - distance, i) for i in devices if i - distance in devices]
    return lax.ppermute(block, axis, route)


def modal_filter(decay_rate, residue, length_total, lag_count):
    decay = decay_rate / length_total
    weight = residue * jnp.sqrt(-jnp.expm1(-2.0 * decay))
    steps = jnp.arange(lag_count, dtype=jnp.float32)

    def add_mode(running, members):
        mode_decay, mode_weight = members
        return (
            running + mode_weight[:, None] * jnp.exp(-mode_decay[:, None] * steps[None, :]),
            None,
        )

    start_value = jnp.zeros((decay_rate.shape[0], lag_count), jnp.float32)
    running, _ = lax.scan(add_mode, start_value, (decay.T, weight.T))
    return running


def split_sizes(total_size):
    outer_size = 2
    while outer_size * outer_size < total_size or total_size % outer_size != 0:
        outer_size += 2
    return (outer_size, total_size // outer_size)


def angles(row_count, col_count, total_size, factor):
    rows_index = jnp.arange(row_count, dtype=jnp.int32)[:, None]
    cols_index = jnp.arange(col_count, dtype=jnp.int32)[None, :]
    wrapped = rows_index * cols_index * factor % total_size
    return wrapped.astype(jnp.float32) * (2.0 * math.pi / total_size)


def forward_spectrum(signal, outer_size, inner_size, total_size):
    channel_count = signal.shape[0]
    half_outer = outer_size // 2
    blocks = signal.reshape(channel_count, half_outer, inner_size)
    outer_angle = angles(outer_size, half_outer, total_size, inner_size)
    outer_table = jnp.concatenate([jnp.cos(outer_angle), -jnp.sin(outer_angle)], axis=0)
    section_one = jnp.einsum("kn,cnp->ckp", outer_table, blocks, precision=HIGHEST)
    real_part = section_one[:, :outer_size]
    imag_part = section_one[:, outer_size:]
    twist = angles(outer_size, inner_size, total_size, 1)
    twist_cos = jnp.cos(twist)
    twist_sin = jnp.sin(twist)
    real_twist = real_part * twist_cos + imag_part * twist_sin
    imag_twist = imag_part * twist_cos - real_part * twist_sin
    inner_angle = angles(inner_size, inner_size, total_size, outer_size)
    inner_cos = jnp.cos(inner_angle)
    inner_sin = jnp.sin(inner_angle)
    inner_table = jnp.concatenate(
        [
            jnp.concatenate([inner_cos, -inner_sin], axis=1),
            jnp.concatenate([inner_sin, inner_cos], axis=1),
        ],
        axis=0,
    )
    joined = jnp.concatenate([real_twist, imag_twist], axis=2)
    return jnp.einsum("ckq,qr->ckr", joined, inner_table, precision=HIGHEST)


def inverse_real(spectrum, outer_size, inner_size, total_size):
    channel_count = spectrum.shape[0]
    half_outer = outer_size // 2
    inner_angle = angles(inner_size, inner_size, total_size, outer_size)
    inner_cos = jnp.cos(inner_angle)
    inner_sin = jnp.sin(inner_angle)
    inner_table = jnp.concatenate(
        [
            jnp.concatenate([inner_cos, inner_sin], axis=1),
            jnp.concatenate([-inner_sin, inner_cos], axis=1),
        ],
        axis=0,
    )
    section_one = jnp.einsum("ckq,qr->ckr", spectrum, inner_table, precision=HIGHEST)
    real_part = section_one[:, :, :inner_size]
    imag_part = section_one[:, :, inner_size:]
    twist = angles(outer_size, inner_size, total_size, 1)
    twist_cos = jnp.cos(twist)
    twist_sin = jnp.sin(twist)
    real_twist = real_part * twist_cos - imag_part * twist_sin
    imag_twist = real_part * twist_sin + imag_part * twist_cos
    outer_angle = angles(half_outer, outer_size, total_size, inner_size)
    outer_table = jnp.concatenate([jnp.cos(outer_angle), -jnp.sin(outer_angle)], axis=1)
    joined = jnp.concatenate([real_twist, imag_twist], axis=1)
    result = jnp.einsum("bk,ckp->cbp", outer_table, joined, precision=HIGHEST) / total_size
    return result.reshape(channel_count, half_outer * inner_size)


def spectral_conv(signal, filter_rows):
    total_size = 2 * signal.shape[1]
    outer_size, inner_size = split_sizes(total_size)
    signal_spec = forward_spectrum(signal, outer_size, inner_size, total_size)
    filter_spec = forward_spectrum(filter_rows, outer_size, inner_size, total_size)
    signal_real = signal_spec[:, :, :inner_size]
    signal_imag = signal_spec[:, :, inner_size:]
    filter_real = filter_spec[:, :, :inner_size]
    filter_imag = filter_spec[:, :, inner_size:]
    joined = jnp.concatenate(
        [
            signal_real * filter_real - signal_imag * filter_imag,
            signal_real * filter_imag + signal_imag * filter_real,
        ],
        axis=2,
    )
    return inverse_real(joined, outer_size, inner_size, total_size)


def shards(query_in, key_in, value_in, short_filter, decay_rate, residue, out_weight):
    row_count, local_width = query_in.shape
    ctx_count = lax.axis_size("ctx")
    tokens_total = row_count * ctx_count
    stacked = jnp.stack([query_in, key_in, value_in])
    border = from_behind(stacked[:, row_count - (SHORT_TAPS - 1) :, :], "ctx", 1)
    extended = jnp.concatenate([border, stacked], axis=1).astype(jnp.float32)
    running = jnp.zeros(stacked.shape, jnp.float32)
    for offset in range(SHORT_TAPS):
        begin = SHORT_TAPS - 1 - offset
        running = (
            running + short_filter[:, offset, None, :] * extended[:, begin : begin + row_count, :]
        )
    featured = jnp.transpose(running, (0, 2, 1)).astype(jnp.bfloat16)
    query_t = featured[0]
    product_t = (featured[1].astype(jnp.float32) * featured[2].astype(jnp.float32)).astype(
        jnp.bfloat16
    )
    slab = lax.all_to_all(product_t, "ctx", split_axis=0, concat_axis=1, tiled=True)
    slab_width = local_width // ctx_count
    first_channel = lax.axis_index("ctx") * slab_width
    slab_rate = lax.dynamic_slice_in_dim(decay_rate, first_channel, slab_width, 0)
    slab_residue = lax.dynamic_slice_in_dim(residue, first_channel, slab_width, 0)
    filter_rows = modal_filter(slab_rate, slab_residue, tokens_total, tokens_total)
    convolved = spectral_conv(slab.astype(jnp.float32), filter_rows)
    long_t = lax.all_to_all(
        convolved.astype(jnp.bfloat16), "ctx", split_axis=1, concat_axis=0, tiled=True
    )
    gated_t = (query_t.astype(jnp.float32) * long_t.astype(jnp.float32)).astype(jnp.bfloat16)
    partial_sums = lax.dot_general(
        gated_t,
        lax.all_gather(out_weight, "ctx", axis=1, tiled=True),
        (((0,), (0,)), ((), ())),
        preferred_element_type=jnp.float32,
    )
    return lax.psum_scatter(partial_sums, "ch", scatter_dimension=0, tiled=True).astype(
        jnp.bfloat16
    )


def solution(mesh):
    return jax.shard_map(
        shards,
        mesh=mesh,
        in_specs=(
            P("ctx", "ch"),
            P("ctx", "ch"),
            P("ctx", "ch"),
            P(None, None, "ch"),
            P("ch", None),
            P("ch", None),
            P("ch", "ctx"),
        ),
        out_specs=P(("ctx", "ch"), None),
        check_vma=False,
    )
```

profile of v0, /device:TPU:1, one launch (start us, length us, event | category | flops | bytes accessed | tf_op | source)
XLA Modules:
  0.0 687.6 jit_solution(3246759382452197225)
XLA Ops:
  6.5 1.1 copy.31
  7.7 1.1 copy.32
  8.8 1.1 copy.33
  9.9 0.3 pad_maximum_fusion
  10.2 0.3 copy.34
  10.5 4.4 collective-permute-start
  14.9 0.0 all-gather.2.cloned.1.call-update
  15.0 0.8 multiply_bitcast_fusion
  15.8 0.0 collective-permute-done
  15.8 0.4 copy.35
  16.3 0.6 maximum_convert_fusion
  16.9 2.4 fusion.33
  19.2 0.8 fusion.41
  20.0 22.3 %all-to-all-start = ((bf16[128,8,128]{2,1,0:T(8,128)(2,1)}), bf16[128,8,128]{2,1,0:T(8,128)(2,1)}, u32[]{:S(2)}, u32[]{:S(2)}) async-start(bf16[128,8,128]{2,1,0:T(8,128)(2,1)} %fusion.41), calls=%async_computation | async-start | bytes 524288 | tf_op jit(solution)/shard_map/all_to_all | solution.py:144
  42.3 0.0 reduce-scatter.2.cloned.1.call-start
  42.4 5.4 while.11
  42.4 0.3 fusion.82
  42.7 0.3 fusion.82
  43.0 0.3 fusion.82
  43.4 0.3 fusion.82
  43.7 0.3 fusion.82
  44.0 0.3 fusion.82
  44.3 0.3 fusion.82
  44.7 0.3 fusion.82
  45.0 0.3 fusion.82
  45.3 0.3 fusion.82
  45.6 0.3 fusion.82
  46.0 0.3 fusion.82
  46.3 0.3 fusion.82
  46.6 0.3 fusion.82
  46.9 0.3 fusion.82
  47.3 0.3 fusion.82
  47.7 0.5 fusion.69
  48.2 0.1 copy.37
  48.3 0.5 fusion.68
  48.8 0.8 copy.38
  49.6 0.9 fusion.72
  50.5 0.9 fusion.70
  51.4 0.5 sine_negate_fusion.1
  52.0 0.0 copy-start.1
  52.0 1.3 sine_negate_fusion
  53.3 1.8 convolution_bitcast_fusion
  55.1 5.9 all-to-all-done
  61.0 1.2 copy.36
  62.2 2.0 convolution_bitcast_fusion.1
  64.2 0.6 multiply_add_fusion.3
  64.8 0.2 copy-done.3
  65.0 0.0 copy-done.4
  65.0 0.0 copy-done.5
  65.1 2.0 fusion.5
  67.1 2.0 fusion.9
  69.1 0.3 multiply_subtract_fusion.1
  69.5 2.3 fusion.13
  71.8 0.3 multiply_subtract_fusion
  72.1 0.6 copy-done.6
  72.7 0.1 copy-done.7
  72.7 1.8 fusion.30
  74.5 0.2 copy.46
  74.7 32.2 %all_to_all.23 = bf16[8,128,128]{2,0,1:T(8,128)(2,1)S(1)} all-to-all(bf16[8,128,128]{2,0,1:T(8,128)(2,1)S(1)} %copy.46), channel_id=1, replica_groups=mesh['ctx'=128,'ch'=4] {'ctx'}, dimensions={1} | all-to-all | bytes 524288 | tf_op jit(solution)/shard_map/all_to_all | solution.py:151
  106.9 436.4 %all-gather.2.cloned.1.call-done = bf16[1024,4096]{0,1:T(8,128)(2,1)} async-done(((bf16[1024,32]{0,1:T(8,128)(2,1)}), bf16[1024,4096]{0,1:T(8,128)(2,1)}) %all-gather.2.cloned.1.call-update) | async-done | bytes 8388624 | tf_op jit(solution)/shard_map/all_gather | solution.py:157
  543.3 7.7 %fusion.42 = f32[128,4096]{1,0:T(8,128)} fusion(bf16[1024,4096]{0,1:T(8,128)(2,1)} %all-gather.2.cloned.1.call-done, bf16[8,128,128]{2,0,1:T(8,128)(2,1)S(1)} %all_to_all.23, bf16[3,1024,128]{2,1,0:T(8,128)(2,1)S(1)} %fusion.33), kind=kOutput, calls=%fused_computation.59 | convolution fusion | flops 1074266112 | bytes 11010048 | tf_op jit(solution)/shard_map/dot_general | solution.py:155
  551.0 0.0 reduce-scatter.2.cloned.1.call-update
  551.0 128.0 %reduce-scatter.2.cloned.1.call-done = f32[32,4096]{1,0:T(8,128)} async-done(((f32[128,4096]{1,0:T(8,128)}), f32[32,4096]{1,0:T(8,128)}) %reduce-scatter.2.cloned.1.call-update) | async-done | bytes 524304 | tf_op jit(solution)/shard_map/reduce_scatter | solution.py:161
  679.0 1.8 convert_element_type.138
  (33 shorter events, 0.2 us)
Async XLA Ops:
  6.5 8.4 %copy-start.8 = (f32[3,3,1024]{2,1,0:T(4,128)S(1)}, f32[3,3,1024]{2,1,0:T(4,128)}, u32[]{:S(2)}) copy-start(f32[3,3,1024]{2,1,0:T(4,128)} %param.12) | copy-start | bytes 110596
  6.5 536.8 %all-gather.2.cloned.1.call-start = ((), (), s32[]{:S(2)}) async-start(), calls=%async_computation.3 | async-start | bytes 8454144 | tf_op jit(solution)/shard_map/all_gather | solution.py:157
  10.5 5.3 collective-permute-start
  20.0 41.0 %all-to-all-start = ((bf16[128,8,128]{2,1,0:T(8,128)(2,1)}), bf16[128,8,128]{2,1,0:T(8,128)(2,1)}, u32[]{:S(2)}, u32[]{:S(2)}) async-start(bf16[128,8,128]{2,1,0:T(8,128)(2,1)} %fusion.41), calls=%async_computation | async-start | bytes 524288 | tf_op jit(solution)/shard_map/all_to_all | solution.py:144
  42.3 636.7 %reduce-scatter.2.cloned.1.call-start = ((), (), s32[]{:S(2)}) async-start(), calls=%async_computation.4 | async-start | bytes 2621440 | tf_op jit(solution)/shard_map/reduce_scatter | solution.py:161
  52.0 1.3 copy-start.1
  52.0 1.3 copy-start.2
  55.1 9.0 %copy-start = (f32[256,128]{0,1:T(8,128)S(1)}, f32[256,128]{0,1:T(8,128)}, u32[]{:S(2)}) copy-start(f32[256,128]{0,1:T(8,128)} %copy.38) | copy-start | bytes 393220
  64.2 0.8 copy-start.3
  64.2 0.9 copy-start.4
  64.2 0.9 copy-start.5
  71.8 0.9 copy-start.6
  71.8 1.0 copy-start.7
Sparse Core Ops, SparseCore 0:
  15.0 528.2 all-gather.1
  551.2 127.8 reduce-scatter.1
where the time goes:
time: 688 us
  waiting for transfers between devices  570 us (83%)
  blocking collectives  32.2 us (5%)
  starting transfers between devices  26.7 us (4%)
  matrix products  19.7 us (3%)
  other arithmetic  17.1 us (2%)
  between operations  13.7 us (2%)
  local copies, waits for them, and re-layouts  7.3 us (1%)
    all_gather x1, waiting for transfers between devices, shards(): lax.all_gather(out_weight, 'ctx', axis=1, tiled=True)  436 us
    reduce_scatter x1, waiting for transfers between devices, shards(): lax.psum_scatter(partial_sums, 'ch', scatter_dimension=0, tiled=True)  128 us
    all_to_all x1, blocking collectives, shards(): lax.all_to_all(convolved.astype(jnp.bfloat16), 'ctx', split_axis=1, conca...  32.2 us
    all_to_all x1, starting transfers between devices, shards(): lax.all_to_all(product_t, 'ctx', split_axis=0, concat_axis=1, tiled=True)  22.3 us
  transfers between devices with their start and end apart: 4, of which 3 were waited for; matrix products, arithmetic and copies ran while one was open for 4% of the time, Pallas kernels for 0%

commit v1 on v0

v1 whole, which is shorter than its diff:
```python
import functools

import jax
import jax.numpy as jnp
from jax import lax
from jax.experimental import pallas as pl
from jax.experimental.pallas import tpu as pltpu
from jax.sharding import PartitionSpec as P

MESH = pl.DeviceIdType.MESH
F32 = jnp.float32
BF16 = jnp.bfloat16

XN, YN, ZN = 2, 4, 16
ROWS = XN * YN
TAPS = 3
MODES = 16
TOK = 128
CHN = 1024
TILES = CHN // 128
SEG = 8
STEPS = TOK // SEG
COLS = 32
RUN = ZN * COLS
QTR = TOK // 4


def rounded(x):
    return x.astype(BF16).astype(F32)


def kernel(
    q_ref, k_ref, v_ref, taps_ref, rate_ref, rate3_ref, weight_ref, wt_ref, out_ref,
    xs, halo_out, halo_in, prod, qconv, local, powers, ends, z_in, before, totals, carry_out, carry_in,
    gate, pooled, wg, part, part_out, part_in, half_out, half_in, done,
    halo_sem, z_sem, row_sem, back_sem, own_sem, other_sem, cross_sem, fore_sem, pool_sem, core_sem, hi_sem, out_sem,
):
    ctx = lax.axis_index("ctx")
    ch = lax.axis_index("ch")
    xl, y, z = ctx // (YN * ZN), (ctx // ZN) % YN, ctx % ZN
    row = ctx // ZN
    hi, core = ch // 2, ch % 2

    def at(xl, y, z):
        return ((xl * YN + y) * ZN + z, ch)

    def send(src, dst, sems, index, device):
        copy = pltpu.make_async_remote_copy(
            src_ref=src,
            dst_ref=dst,
            send_sem=sems.at[0, index],
            recv_sem=sems.at[1, index],
            device_id=device,
            device_id_type=MESH,
        )
        return copy

    nxt = ((ctx + 1) % (XN * YN * ZN), ch)
    prv = ((ctx + XN * YN * ZN - 1) % (XN * YN * ZN), ch)
    mate = (ctx, hi * 2 + 1 - core)
    far = (ctx, (1 - hi) * 2 + core)
    z_up, z_down = at(xl, y, (z + 1) % ZN), at(xl, y, (z + ZN - 1) % ZN)
    y_up, y_down = at(xl, (y + 1) % YN, z), at(xl, (y + YN - 1) % YN, z)
    y_far = at(xl, (y + 2) % YN, z)
    x_mate = at(1 - xl, y, z)

    barrier = pltpu.get_barrier_semaphore()

    def greet(device):
        pl.semaphore_signal(barrier, inc=1, device_id=device, device_id_type=MESH)

    for device in (nxt, prv, mate, far):
        greet(device)

    @pl.loop(1, ZN)
    def _(o):
        greet((row * ZN + (z + o) % ZN, ch))

    @pl.loop(1, ROWS)
    def _(o):
        greet((((row + o) % ROWS) * ZN + z, ch))

    streams = (q_ref, k_ref, v_ref)
    halo_out[...] = jnp.zeros_like(halo_out)
    for s, stream in enumerate(streams):
        halo_out[2 * s : 2 * s + 2, :] = stream[TOK - 16 :, :].astype(F32)[14:16]
    pl.semaphore_wait(barrier, 4 + (ZN - 1) + (ROWS - 1))

    started = []

    def go(copy):
        copy.start()
        started.append(copy)
        return copy

    halo = go(send(halo_out, halo_in, halo_sem, 0, nxt))

    wg[xl, z] = wt_ref[...]
    lower, upper = pl.ds(0, COLS // 2), pl.ds(COLS // 2, COLS // 2)

    def block(side, index, part_rows=None):
        ref = wg.at[side, lax.rem(index + 2 * ZN, ZN)]
        return ref if part_rows is None else ref.at[part_rows]

    HALF = ZN // 2
    own_up, own_down, other_up, other_down, fore = {}, {}, {}, {}, {}

    def start_own(step):
        if step < HALF:
            own_up[step] = go(send(block(xl, z - step), block(xl, z - step), own_sem, step, z_up))
        if step < HALF - 1:
            own_down[step] = go(
                send(block(xl, z + step), block(xl, z + step), own_sem, HALF + step, z_down)
            )

    def start_other(step):
        if step < HALF - 1:
            b = block(1 - xl, z - step, upper)
            other_up[step] = go(send(b, b, other_sem, step, z_up))
        if step < HALF:
            b = block(1 - xl, z + step, upper)
            other_down[step] = go(send(b, b, other_sem, HALF + step, z_down))

    def forward(name, index):
        b = block(xl, index, lower)
        fore[name] = go(send(b, b, fore_sem, name, x_mate))

    start_own(0)
    b = block(xl, z, upper)
    cross = go(send(b, b, cross_sem, 0, x_mate))
    forward(0, z)

    def tick(step):
        if step - 1 in own_up:
            own_up[step - 1].wait_recv()
        if step - 1 in own_down:
            own_down[step - 1].wait_recv()
        if step == 0:
            cross.wait_recv()
        else:
            start_own(step)
            if step - 1 in other_up:
                other_up[step - 1].wait_recv()
            if step - 1 in other_down:
                other_down[step - 1].wait_recv()
        start_other(step)
        if 1 <= step <= HALF:
            forward(step, z - step)
        if 1 <= step <= HALF - 1:
            forward(HALF + step, z + step)

    for s, stream in enumerate(streams):
        for j in range(TILES):
            xs[s, j, 8:, :] = stream[:, j * 128 : (j + 1) * 128].astype(F32)

    def convolved(s, j, i, x0, x1, x2):
        taps = taps_ref[j]
        f = [taps[s * TAPS + t : s * TAPS + t + 1] for t in range(TAPS)]
        return rounded((f[0] * x0 + f[1] * x1) + f[2] * x2)

    def features(j, first, last):
        prev = {}
        for s in range(3):
            prev[s] = [
                xs[s, j, pl.ds(8 + first - d, SEG, stride=STEPS), :] for d in (1, 2)
            ]
        for i in range(first, last):
            out = []
            for s in range(3):
                x0 = xs[s, j, pl.ds(8 + i, SEG, stride=STEPS), :]
                x1, x2 = prev[s]
                out.append(convolved(s, j, i, x0, x1, x2))
                prev[s] = [x0, x1]
            qconv[j, i] = out[0]
            prod[j, i] = rounded(out[1] * out[2])

    @pl.loop(0, TILES)
    def _(j):
        features(j, 2, STEPS)

    tick(0)

    halo.wait_recv()
    seen = jnp.where(ctx == 0, 0.0, 1.0).astype(F32)
    for s in range(3):
        for j in range(TILES):
            xs[s, j, 6:8, :] = halo_in[2 * s : 2 * s + 2, j * 128 : (j + 1) * 128] * seen

    segment = lax.broadcasted_iota(jnp.int32, (SEG, 128), 0)

    @pl.loop(0, TILES)
    def _(j):
        features(j, 0, 2)
        rate = rate_ref[j]
        keep = jnp.exp(-rate)
        decays = [jnp.broadcast_to(keep[n : n + 1], (SEG, 128)) for n in range(MODES)]
        states = [jnp.zeros((SEG, 128), F32) for _ in range(MODES)]
        for i in range(STEPS):
            p = prod[j, i]
            states = [d * st + p for d, st in zip(decays, states)]
        for n in range(MODES):
            a = rate[n : n + 1]
            total = states[n]
            for k in (1, 2, 4):
                moved = jnp.where(segment >= k, pltpu.roll(total, k, 0), 0.0)
                total = total + jnp.exp(a * (-float(STEPS * k))) * moved
            local[j, n] = jnp.where(segment >= 1, pltpu.roll(total, 1, 0), 0.0)
            powers[j, n] = jnp.exp(a * (segment * -STEPS).astype(F32))
            ends[n, pl.ds(j, 1), :] = total[SEG - 1 : SEG]

    def z_copy(o):
        to = (z + o) % ZN
        return send(ends.at[to], z_in.at[z], z_sem, o, (row * ZN + to, ch))

    @pl.loop(1, ZN)
    def _(o):
        z_copy(o).start()

    z_in[z] = ends[z]
    tick(1)

    @pl.loop(1, ZN)
    def _(o):
        z_copy(o).wait_recv()

    rate = rate3_ref[z]
    keep = jnp.exp(rate * -float(TOK))
    state = jnp.zeros((SEG, 128), F32)
    for zz in range(ZN):
        before[zz] = state
        state = keep * state + z_in[zz]
    totals[row] = state

    def row_copy(o):
        to = (row + o) % ROWS
        return send(totals.at[row], totals.at[row], row_sem, o, (to * ZN + z, ch))

    @pl.loop(1, ROWS)
    def _(o):
        row_copy(o).start()

    tick(2)

    @pl.loop(1, ROWS)
    def _(o):
        row_copy(o).wait_recv()

    keep_row = jnp.exp(rate * -float(TOK * ZN))
    state = jnp.zeros((SEG, 128), F32)
    for r in range(ROWS):
        state = jnp.where(r < row, keep_row * state + totals[r], state)
    for zz in range(ZN):
        carry_out[zz] = before[zz] + state
        state = keep * state

    def back_copy(o):
        to = (z + o) % ZN
        return send(carry_out.at[to], carry_in.at[z], back_sem, o, (row * ZN + to, ch))

    @pl.loop(1, ZN)
    def _(o):
        back_copy(o).start()

    carry_in[z] = carry_out[z]
    tick(3)

    @pl.loop(1, ZN)
    def _(o):
        back_copy(o).wait_recv()

    @pl.loop(0, TILES)
    def _(j):
        keep = jnp.exp(-rate_ref[j])
        weight = weight_ref[j]
        decays = [jnp.broadcast_to(keep[n : n + 1], (SEG, 128)) for n in range(MODES)]
        weights = [jnp.broadcast_to(weight[n : n + 1], (SEG, 128)) for n in range(MODES)]
        states = [
            local[j, n] + powers[j, n] * carry_in[n, pl.ds(j, 1), :] for n in range(MODES)
        ]
        for i in range(STEPS):
            p = prod[j, i]
            states = [d * st + p for d, st in zip(decays, states)]
            terms = [w * st for w, st in zip(weights, states)]
            while len(terms) > 1:
                terms = [a + b for a, b in zip(terms[::2], terms[1::2])]
            gate[j, pl.ds(i, SEG, stride=STEPS), :] = qconv[j, i] * rounded(terms[0])

    for j in range(TILES):
        pooled[0, :, j * 128 : (j + 1) * 128] = gate[j].astype(BF16)

    top, bottom = pl.ds(0, TOK // 2), pl.ds(TOK // 2, TOK // 2)

    def pool(slot, to_slot, rows, index, device):
        return go(send(pooled.at[slot, rows], pooled.at[to_slot, rows], pool_sem, index, device))

    up_a = pool(0, 1, top, 0, y_up)
    down_a = pool(0, 2, bottom, 1, y_down)
    up_b = pool(0, 1, bottom, 2, y_up)
    down_b = pool(0, 2, top, 3, y_down)

    for step in range(4, HALF + 1):
        tick(step)
    up_a.wait_recv()
    up_far = pool(1, 3, top, 4, y_up)
    down_a.wait_recv()
    down_far = pool(2, 3, bottom, 5, y_down)
    for copy in fore.values():
        copy.wait_recv()

    owners = (None, y_down, y_up, y_far)
    to_core, to_hi = {}, {}

    def project(b):
        for side in range(XN):
            sums = lax.dot_general(
                pooled[b],
                wg[side].reshape(RUN, CHN),
                (((1,), (1,)), ((), ())),
                preferred_element_type=F32,
            )
            for h in range(2):
                for c in range(2):
                    quarter = sums[(h * 2 + c) * QTR : (h * 2 + c + 1) * QTR]
                    part[b, c, h, side] = quarter
                    part_out[b, c, h, side] = quarter.astype(BF16)
        to_core[b] = go(send(part_out.at[b, 1 - core], part_in.at[b], core_sem, b, mate))

    def add_core(b):
        to_core[b].wait_recv()
        half_out[b] = (part[b, core, 1 - hi] + part_in[b, 1 - hi].astype(F32)).astype(BF16)
        to_hi[b] = go(send(half_out.at[b], half_in.at[b], hi_sem, b, far))

    def finish(b):
        to_hi[b].wait_recv()
        mixed = part[b, core, hi] + part_in[b, hi].astype(F32) + half_in[b].astype(F32)
        done[b] = mixed.astype(BF16)
        for side in range(XN):
            columns = pl.ds(pl.multiple_of(side * (YN * RUN) + y * RUN, RUN), RUN)
            if b == 0:
                out_ref[:, columns] = done[b, side]
            else:
                go(send(done.at[b, side], out_ref.at[:, columns], out_sem, b * XN + side, owners[b]))

    project(0)
    up_b.wait_recv()
    project(1)
    add_core(0)
    down_b.wait_recv()
    project(2)
    add_core(1)
    finish(0)
    up_far.wait_recv()
    down_far.wait_recv()
    project(3)
    add_core(2)
    finish(1)
    add_core(3)
    finish(2)
    finish(3)

    @pl.loop(1, ZN)
    def _(o):
        z_copy(o).wait_send()
        back_copy(o).wait_send()

    @pl.loop(1, ROWS)
    def _(o):
        row_copy(o).wait_send()

    for copy in started:
        copy.wait_send()

    for b, owner in ((1, y_up), (2, y_down), (3, y_far)):
        sender = (y + {1: 1, 2: YN - 1, 3: 2}[b]) % YN
        for side in range(XN):
            columns = pl.ds(pl.multiple_of(side * (YN * RUN) + sender * RUN, RUN), RUN)
            send(done.at[b, side], out_ref.at[:, columns], out_sem, b * XN + side, owner).wait_recv()


def shards(query_in, key_in, value_in, short_filter, decay_rate, residue, out_weight):
    tokens_total = TOK * XN * YN * ZN
    decay = decay_rate / tokens_total
    weight = residue * jnp.sqrt(-jnp.expm1(-2.0 * decay))
    rate = jnp.transpose(decay.reshape(TILES, 128, MODES), (0, 2, 1))
    rate3 = jnp.transpose(rate, (1, 0, 2))
    weight = jnp.transpose(weight.reshape(TILES, 128, MODES), (0, 2, 1))
    taps = jnp.transpose(short_filter.reshape(3 * TAPS, TILES, 128), (1, 0, 2))
    vmem = pl.BlockSpec(memory_space=pltpu.VMEM)

    def sems(count):
        return pltpu.SemaphoreType.DMA((2, count))

    half = ZN // 2
    return pl.pallas_call(
        kernel,
        out_shape=jax.ShapeDtypeStruct((QTR, 4096), BF16),
        in_specs=[vmem] * 8,
        out_specs=vmem,
        scratch_shapes=[
            pltpu.VMEM((3, TILES, 8 + TOK, 128), F32),
            pltpu.VMEM((8, CHN), F32),
            pltpu.VMEM((8, CHN), F32),
            pltpu.VMEM((TILES, STEPS, SEG, 128), F32),
            pltpu.VMEM((TILES, STEPS, SEG, 128), F32),
            pltpu.VMEM((TILES, MODES, SEG, 128), F32),
            pltpu.VMEM((TILES, MODES, SEG, 128), F32),
            pltpu.VMEM((MODES, TILES, 128), F32),
            pltpu.VMEM((ZN, TILES, 128), F32),
            pltpu.VMEM((ZN, TILES, 128), F32),
            pltpu.VMEM((ROWS, TILES, 128), F32),
            pltpu.VMEM((ZN, TILES, 128), F32),
            pltpu.VMEM((MODES, TILES, 128), F32),
            pltpu.VMEM((TILES, TOK, 128), F32),
            pltpu.VMEM((YN, TOK, CHN), BF16),
            pltpu.VMEM((XN, ZN, COLS, CHN), BF16),
            pltpu.VMEM((YN, 2, 2, XN, QTR, RUN), F32),
            pltpu.VMEM((YN, 2, 2, XN, QTR, RUN), BF16),
            pltpu.VMEM((YN, 2, XN, QTR, RUN), BF16),
            pltpu.VMEM((YN, XN, QTR, RUN), BF16),
            pltpu.VMEM((YN, XN, QTR, RUN), BF16),
            pltpu.VMEM((YN, XN, QTR, RUN), BF16),
            sems(1),
            sems(ZN),
            sems(ROWS),
            sems(ZN),
            sems(2 * half),
            sems(2 * half),
            sems(1),
            sems(ZN),
            sems(6),
            sems(YN),
            sems(YN),
            sems(YN * XN),
        ],
        compiler_params=pltpu.CompilerParams(
            collective_id=0, has_side_effects=True, vmem_limit_bytes=40 * 1024 * 1024
        ),
        cost_estimate=pl.CostEstimate(
            flops=2 * 4 * TOK * CHN * CHN, bytes_accessed=4 * 1024 * 1024, transcendentals=0
        ),
    )(query_in, key_in, value_in, taps, rate, rate3, weight, jnp.transpose(out_weight))


def solution(mesh):
    return jax.shard_map(
        shards,
        mesh=mesh,
        in_specs=(
            P("ctx", "ch"),
            P("ctx", "ch"),
            P("ctx", "ch"),
            P(None, None, "ch"),
            P("ch", None),
            P("ch", None),
            P("ch", "ctx"),
        ),
        out_specs=P(("ctx", "ch"), None),
        check_vma=False,
    )
```

time: 688 us -> 85 us (0.12)
  waiting for transfers between devices: 570 us -> 0 us
  Pallas kernels: 0 us -> 81.2 us
  blocking collectives: 32.2 us -> 0 us
  starting transfers between devices: 26.7 us -> 0 us
  matrix products: 19.7 us -> 0 us
  other arithmetic: 17.1 us -> 0.97 us
  between operations: 13.7 us -> 0.09 us
    all_gather x1 -> x0, waiting for transfers between devices: 436 us -> none  [shards(): lax.all_gather(out_weight, 'ctx', axis=1, tiled=True)]
    reduce_scatter x1 -> x0, waiting for transfers between devices: 128 us -> none  [shards(): lax.psum_scatter(partial_sums, 'ch', scatter_dimension=0, tiled=True)]
    pallas_call x0 -> x1, Pallas kernels: none -> 81.2 us  [shards(): pl.pallas_call(kernel, out_shape=jax.ShapeDtypeStruct((QTR, 4096), BF16),...]
    all_to_all x1 -> x0, blocking collectives: 32.2 us -> none  [shards(): lax.all_to_all(convolved.astype(jnp.bfloat16), 'ctx', split_axis=1, conca...]
    all_to_all x1 -> x0, starting transfers between devices: 22.3 us -> none  [shards(): lax.all_to_all(product_t, 'ctx', split_axis=0, concat_axis=1, tiled=True)]
    dot_general x7 -> x0, matrix products: 19.7 us -> none  [the longest x1 7.71 us: shards(): lax.dot_general(gated_t, lax.all_gather(out_weight, 'ctx', axis=1, tiled=...]
  transfers between devices with their start and end apart: 4 -> 0, of which waited for: 3 -> 0; matrix products, arithmetic and copies ran while one was open for 4% -> 0% of each run, Pallas kernels for 0% -> 0%
where the time goes in v1:
time: 85 us; the launch traced here: 84.8 us
  Pallas kernels  81.2 us (96%)
  local copies, waits for them, and re-layouts  2.5 us (3%)
  other arithmetic  0.97 us (1%)
    pallas_call x1, Pallas kernels, shards(): pl.pallas_call(kernel, out_shape=jax.ShapeDtypeStruct((QTR, 4096), BF16),...  81.2 us

profile of v1, /device:TPU:1, one launch (start us, length us, event | category | flops | bytes accessed | tf_op | source)
XLA Modules:
  0.0 84.8 jit_solution(15625579305970441027)
XLA Ops:
  0.0 0.0 copy-start.2
  0.0 0.9 %reshape.9 = f32[9,8,128]{2,1,0:T(8,128)S(1)} reshape(f32[3,3,1024]{2,1,0:T(4,128)} %param.10) | data formatting | bytes 73728 | tf_op jit(solution)/shard_map/reshape | solution.py:387
  0.9 0.0 copy-start.1
  0.9 1.0 %multiply_bitcast_fusion = (f32[2,8,8,128]{3,2,1,0:T(8,128)S(1)}, f32[2,8,8,128]{3,1,2,0:T(8,128)S(1)}) fusion(f32[1024,16]{0,1:T(8,128)} %param.12, f32[1024,16]{0,1:T(8,128)} %param.11), kind=kLoop, calls=%fused_computation.2 | loop fusion | flops 65536 | bytes 262144
  1.9 0.0 copy-start
  1.9 0.0 copy-start.3
  2.0 0.0 copy-done.2
  2.0 0.0 copy-done.1
  2.0 0.9 %copy-done = bf16[128,1024]{1,0:T(8,128)(2,1)S(1)} copy-done((bf16[128,1024]{1,0:T(8,128)(2,1)S(1)}, bf16[128,1024]{1,0:T(8,128)(2,1)}, u32[]{:S(2)}) %copy-start) | copy-done | bytes 262168
  2.8 0.0 copy-done.3
  2.8 81.2 %shard_map.73 = bf16[32,4096]{1,0:T(8,128)(2,1)S(1)} custom-call(bf16[128,1024]{1,0:T(8,128)(2,1)S(1)} %copy-done, bf16[128,1024]{1,0:T(8,128)(2,1)S(1)} %copy-done.1, bf16[128,1024]{1,0:T(8,128)(2,1)S(1)} %copy-done.2, f32[8,9,128]{2,1,0:T(8,128)S(1)} %bitcast.23, f32[8,16,128]{2,1,0:T(8,128)S(1)} %copy.11.rate_ref, f32[16,8,128]{2,1,0:T(8,128)S(1)} %bitcast.22, ...), custom_call_target="tpu_custom_call" | custom-call | flops 1073741824 | bytes 4194304 | tf_op jit(solution)/shard_map/pallas_call | solution.py:394
  84.1 0.7 copy.19
  (4 shorter events, 0.0 us)
Async XLA Ops:
  0.0 2.0 %copy-start.2 = (bf16[128,1024]{1,0:T(8,128)(2,1)S(1)}, bf16[128,1024]{1,0:T(8,128)(2,1)}, u32[]{:S(2)}) copy-start(bf16[128,1024]{1,0:T(8,128)(2,1)} %v_ref.1) | copy-start | bytes 786436
  0.9 1.1 %copy-start.1 = (bf16[128,1024]{1,0:T(8,128)(2,1)S(1)}, bf16[128,1024]{1,0:T(8,128)(2,1)}, u32[]{:S(2)}) copy-start(bf16[128,1024]{1,0:T(8,128)(2,1)} %k_ref.1) | copy-start | bytes 786436
  1.9 1.0 %copy-start = (bf16[128,1024]{1,0:T(8,128)(2,1)S(1)}, bf16[128,1024]{1,0:T(8,128)(2,1)}, u32[]{:S(2)}) copy-start(bf16[128,1024]{1,0:T(8,128)(2,1)} %q_ref.1) | copy-start | bytes 786436
  1.9 0.9 %copy-start.3 = (bf16[1024,32]{0,1:T(8,128)(2,1)S(1)}, bf16[1024,32]{0,1:T(8,128)(2,1)}, u32[]{:S(2)}) copy-start(bf16[1024,32]{0,1:T(8,128)(2,1)} %param.13) | copy-start | bytes 196612

commit v2 on v1

v2 whole, which is shorter than its diff:
```python
import jax
import jax.numpy as jnp
from jax import lax
from jax.experimental import pallas as pl
from jax.experimental.pallas import tpu as pltpu
from jax.sharding import PartitionSpec as P

MESH = pl.DeviceIdType.MESH
F32 = jnp.float32
BF16 = jnp.bfloat16

XN, YN, ZN = 2, 4, 16
ROWS = XN * YN
TAPS = 3
MODES = 16
TOK = 128
CHN = 1024
TILES = CHN // 128
SEG = 8
STEPS = TOK // SEG
COLS = 32
RUN = ZN * COLS
QTR = TOK // 4
HALF = ZN // 2
LENGTH = TOK * XN * YN * ZN


def rounded(x):
    return x.astype(BF16).astype(F32)


def mode_weight(rate, residue):
    square = rate * rate
    series = rate * (1.0 + square * (1.0 / 6.0 + square * (1.0 / 120.0 + square * (1.0 / 5040.0))))
    small = 2.0 * jnp.exp(-rate) * series
    large = 1.0 - jnp.exp(-2.0 * rate)
    return residue * jnp.sqrt(jnp.where(rate < 0.25, small, large))


def kernel(
    q_hbm, k_hbm, v_hbm, taps_hbm, rate_hbm, residue_hbm, wt_hbm, out_ref,
    q_in, k_in, v_in, taps_in, rate_in, residue_in, wt_in,
    taps, rates, keeps, weights, line_rate,
    xs, halo_out, halo_in, prod, qconv, local, powers, ends_own, ends, z_in, before, totals, carry_out, carry_in,
    gate, pooled, wg, part, part_out, part_in, last_out, last_in,
    load_sem, halo_sem, z_sem, row_sem, back_sem, ring_sem, cross_sem, fore_sem, pool_sem, core_sem, last_sem,
):
    ctx = lax.axis_index("ctx")
    ch = lax.axis_index("ch")
    xl, y, z = ctx // (YN * ZN), (ctx // ZN) % YN, ctx % ZN
    row = ctx // ZN
    hi, core = ch // 2, ch % 2

    loads = []
    for i, (src, dst) in enumerate(
        (
            (k_hbm, k_in), (v_hbm, v_in), (q_hbm, q_in), (wt_hbm, wt_in),
            (rate_hbm, rate_in), (taps_hbm, taps_in), (residue_hbm, residue_in),
        )
    ):
        loads.append(pltpu.make_async_copy(src, dst, load_sem.at[i]))
        loads[-1].start()

    def at(xl, y, z, ch=ch):
        return ((xl * YN + y) * ZN + z, ch)

    def send(src, dst, sems, index, device):
        return pltpu.make_async_remote_copy(
            src_ref=src,
            dst_ref=dst,
            send_sem=sems.at[0, index],
            recv_sem=sems.at[1, index],
            device_id=device,
            device_id_type=MESH,
        )

    nxt = ((ctx + 1) % (XN * YN * ZN), ch)
    prv = ((ctx + XN * YN * ZN - 1) % (XN * YN * ZN), ch)
    mate = (ctx, hi * 2 + 1 - core)
    far_ch = (1 - hi) * 2 + core
    z_up, z_down = at(xl, y, (z + 1) % ZN), at(xl, y, (z + ZN - 1) % ZN)
    y_of = (y, (y + YN - 1) % YN, (y + 1) % YN, (y + 2) % YN)
    y_down, y_up = at(xl, y_of[1], z), at(xl, y_of[2], z)
    x_mate = at(1 - xl, y, z)

    barrier = pltpu.get_barrier_semaphore()

    def greet(device):
        pl.semaphore_signal(barrier, inc=1, device_id=device, device_id_type=MESH)

    @pl.loop(1, ZN)
    def _(o):
        greet((row * ZN + (z + o) % ZN, ch))

    for device in (nxt, prv, mate):
        greet(device)
    for b in range(YN):
        greet(at(xl, y_of[b], z, far_ch))

    @pl.loop(1, ROWS)
    def _(o):
        greet((((row + o) % ROWS) * ZN + z, ch))

    halo_out[...] = jnp.zeros_like(halo_out)
    loads[0].wait()
    loads[1].wait()
    loads[2].wait()
    streams = (q_in, k_in, v_in)
    for s, stream in enumerate(streams):
        halo_out[2 * s : 2 * s + 2, :] = stream[TOK - 16 :, :].astype(F32)[14:16]
    loads[3].wait()
    wg[xl, z] = wt_in[...]
    pl.semaphore_wait(barrier, 3 + YN + (ZN - 1) + (ROWS - 1))

    started = []

    def go(copy):
        copy.start()
        started.append(copy)
        return copy

    halo = go(send(halo_out, halo_in, halo_sem, 0, nxt))

    lower, upper = pl.ds(0, COLS // 2), pl.ds(COLS // 2, COLS // 2)
    chunks = ((xl, upper), (xl, lower), (1 - xl, upper))
    ups, downs, fore = {}, {}, {}

    def piece(side, rows, index):
        return wg.at[side, lax.rem(index + 2 * ZN, ZN), rows]

    def pass_on(step, c):
        side, rows = chunks[c]
        if step < HALF - 1 or (step == HALF - 1 and c < 2):
            b = piece(side, rows, z - step)
            ups[step, c] = go(send(b, b, ring_sem, step * 3 + c, z_up))
        if step < HALF - 1 or (step == HALF - 1 and c == 2):
            b = piece(side, rows, z + step)
            downs[step, c] = go(send(b, b, ring_sem, (HALF + step) * 3 + c, z_down))

    def forward(name, index):
        b = piece(xl, lower, index)
        fore[name] = go(send(b, b, fore_sem, name, x_mate))

    b = piece(xl, upper, z)
    cross = go(send(b, b, cross_sem, 0, x_mate))
    pass_on(0, 0)
    pass_on(0, 1)
    forward(0, z)

    def tick(step):
        for c in range(3):
            if step == 0:
                if c == 2:
                    cross.wait_recv()
                    pass_on(0, 2)
                continue
            if (step - 1, c) in ups:
                ups[step - 1, c].wait_recv()
            if (step - 1, c) in downs:
                downs[step - 1, c].wait_recv()
            if step < HALF:
                pass_on(step, c)
            if c == 1:
                forward(step, z - step)
                if step < HALF:
                    forward(HALF + step, z + step)

    loads[4].wait()
    loads[5].wait()
    loads[6].wait()
    for j in range(TILES):
        lanes = slice(j * 128, (j + 1) * 128)
        rate = rate_in[:, lanes] * (1.0 / LENGTH)
        rates[j] = rate
        keeps[j] = jnp.exp(-rate)
        weights[j] = mode_weight(rate, residue_in[:, lanes])
        for s in range(3):
            for t in range(TAPS):
                taps[j, s * TAPS + t : s * TAPS + t + 1, :] = taps_in[s, t : t + 1, lanes]
        line_rate[j : j + 1, :] = rates[j, pl.ds(z, 1), :]
        for s, stream in enumerate(streams):
            xs[s, j, :8, :] = jnp.zeros((8, 128), F32)
            xs[s, j, 8:, :] = stream[:, lanes].astype(F32)

    def features(j, first, last):
        tap = taps[j]
        prev = [
            [xs[s, j, pl.ds(8 + first - d, SEG, stride=STEPS), :] for d in (1, 2)] for s in range(3)
        ]
        products = []
        for i in range(first, last):
            out = []
            for s in range(3):
                f = [tap[s * TAPS + t : s * TAPS + t + 1] for t in range(TAPS)]
                x0 = xs[s, j, pl.ds(8 + i, SEG, stride=STEPS), :]
                x1, x2 = prev[s]
                out.append(rounded((f[0] * x0 + f[1] * x1) + f[2] * x2))
                prev[s] = [x0, x1]
            qconv[j, i] = out[0]
            p = rounded(out[1] * out[2])
            prod[j, i] = p
            products.append(p)
        return products

    segment = lax.broadcasted_iota(jnp.int32, (SEG, 128), 0)
    later = segment >= 1

    @pl.loop(0, TILES)
    def _(j):
        features(j, 0, STEPS)

    tick(0)

    @pl.loop(0, TILES)
    def _(j):
        rate = rates[j]
        keep = keeps[j]
        decays = [jnp.broadcast_to(keep[n : n + 1], (SEG, 128)) for n in range(MODES)]
        states = [jnp.zeros((SEG, 128), F32) for _ in range(MODES)]
        for i in range(STEPS):
            p = prod[j, i]
            if i < TAPS - 1:
                p = jnp.where(later, p, 0.0)
            states = [d * st + p for d, st in zip(decays, states)]
        for n in range(MODES):
            a = rate[n : n + 1]
            total = states[n]
            for k in (1, 2, 4):
                moved = jnp.where(segment >= k, pltpu.roll(total, k, 0), 0.0)
                total = total + jnp.exp(a * (-float(STEPS * k))) * moved
            local[j, n] = jnp.where(later, pltpu.roll(total, 1, 0), 0.0)
            ends_own[j, n : n + 1, :] = total[SEG - 1 : SEG]

    halo.wait_recv()
    seen = jnp.where(ctx == 0, 0.0, 1.0).astype(F32)
    for s in range(3):
        for j in range(TILES):
            xs[s, j, 6:8, :] = halo_in[2 * s : 2 * s + 2, j * 128 : (j + 1) * 128] * seen

    def first_two(j):
        rate = rates[j]
        return prod[j, 0, 0:1] * jnp.exp(rate) + prod[j, 1, 0:1] * jnp.exp(2.0 * rate)

    @pl.loop(0, TILES)
    def _(j):
        features(j, 0, TAPS - 1)
        total = ends_own[j] + jnp.exp(rates[j] * -float(TOK)) * first_two(j)
        for n in range(MODES):
            ends[n, pl.ds(j, 1), :] = total[n : n + 1]

    def z_copy(o):
        to = (z + o) % ZN
        return send(ends.at[to], z_in.at[z], z_sem, o, (row * ZN + to, ch))

    @pl.loop(1, ZN)
    def _(o):
        z_copy(o).start()

    z_in[z] = ends[z]
    tick(1)

    @pl.loop(0, TILES)
    def _(j):
        rate = rates[j]
        extra = first_two(j)
        for n in range(MODES):
            power = jnp.exp(rate[n : n + 1] * (segment * -STEPS).astype(F32))
            powers[j, n] = power
            local[j, n] = local[j, n] + jnp.where(later, power * extra[n : n + 1], 0.0)

    tick(2)

    @pl.loop(1, ZN)
    def _(o):
        z_copy(o).wait_recv()

    rate = line_rate[...]
    keep = jnp.exp(rate * -float(TOK))
    state = jnp.zeros((SEG, 128), F32)
    for zz in range(ZN):
        before[zz] = state
        state = keep * state + z_in[zz]
    totals[row] = state

    def row_copy(o):
        to = (row + o) % ROWS
        return send(totals.at[row], totals.at[row], row_sem, o, (to * ZN + z, ch))

    @pl.loop(1, ROWS)
    def _(o):
        row_copy(o).start()

    tick(3)

    @pl.loop(1, ROWS)
    def _(o):
        row_copy(o).wait_recv()

    keep_row = jnp.exp(rate * -float(TOK * ZN))
    state = jnp.zeros((SEG, 128), F32)
    for r in range(ROWS):
        state = jnp.where(r < row, keep_row * state + totals[r], state)
    for zz in range(ZN):
        carry_out[zz] = before[zz] + state
        state = keep * state

    def back_copy(o):
        to = (z + o) % ZN
        return send(carry_out.at[to], carry_in.at[z], back_sem, o, (row * ZN + to, ch))

    @pl.loop(1, ZN)
    def _(o):
        back_copy(o).start()

    carry_in[z] = carry_out[z]
    tick(4)
    tick(5)

    @pl.loop(1, ZN)
    def _(o):
        back_copy(o).wait_recv()

    def gated(half):
        @pl.loop(half * (TILES // 2), (half + 1) * (TILES // 2))
        def _(j):
            keep = keeps[j]
            weight = weights[j]
            decays = [jnp.broadcast_to(keep[n : n + 1], (SEG, 128)) for n in range(MODES)]
            scales = [jnp.broadcast_to(weight[n : n + 1], (SEG, 128)) for n in range(MODES)]
            states = [
                local[j, n] + powers[j, n] * carry_in[n, pl.ds(j, 1), :] for n in range(MODES)
            ]
            for i in range(STEPS):
                p = prod[j, i]
                states = [d * st + p for d, st in zip(decays, states)]
                terms = [w * st for w, st in zip(scales, states)]
                while len(terms) > 1:
                    terms = [a + b for a, b in zip(terms[::2], terms[1::2])]
                gate[j, pl.ds(i, SEG, stride=STEPS), :] = qconv[j, i] * rounded(terms[0])

        for i in range(TILES // 2):
            lanes = slice(i * 128, (i + 1) * 128)
            pooled[0, half, :, lanes] = gate[half * (TILES // 2) + i].astype(BF16)

    def pool(slot, to_slot, half, index, device):
        return go(send(pooled.at[slot, half], pooled.at[to_slot, half], pool_sem, index, device))

    gated(0)
    up_a = pool(0, 1, 0, 0, y_up)
    gated(1)
    down_a = pool(0, 2, 1, 1, y_down)
    up_b = pool(0, 1, 1, 2, y_up)
    down_b = pool(0, 2, 0, 3, y_down)

    tick(6)
    tick(7)
    up_a.wait_recv()
    up_far = pool(1, 3, 0, 4, y_up)
    down_a.wait_recv()
    down_far = pool(2, 3, 1, 5, y_down)
    tick(8)
    for copy in fore.values():
        copy.wait_recv()

    to_core, to_owner = {}, {}

    def project(b):
        for side in range(XN):
            sums = 0.0
            for half in range(2):
                depth = slice(half * (CHN // 2), (half + 1) * (CHN // 2))
                sums = sums + lax.dot_general(
                    pooled[b, half],
                    wg[side, :, :, depth].reshape(RUN, CHN // 2),
                    (((1,), (1,)), ((), ())),
                    preferred_element_type=F32,
                )
            for h in range(2):
                for c in range(2):
                    quarter = sums[(h * 2 + c) * QTR : (h * 2 + c + 1) * QTR]
                    part[b, c, h, side] = quarter
                    part_out[b, c, h, side] = quarter.astype(BF16)
        to_core[b] = go(send(part_out.at[b, 1 - core], part_in.at[b], core_sem, b, mate))

    def add_core(b):
        to_core[b].wait_recv()
        for same, h in ((0, hi), (1, 1 - hi)):
            sums = part[b, core, h] + part_in[b, h].astype(F32)
            last_out[b, same] = sums.astype(BF16)
            if b == 0 and same == 0:
                last_in[0, 0] = sums.astype(BF16)
            else:
                to_owner[b, same] = go(
                    send(
                        last_out.at[b, same], last_in.at[b, same], last_sem, b * 2 + same,
                        at(xl, y_of[b], z, h * 2 + core),
                    )
                )

    def finish(b):
        for same in range(2):
            if (b, same) in to_owner:
                to_owner[b, same].wait_recv()
        mixed = last_in[b, 0].astype(F32) + last_in[b, 1].astype(F32)
        sender = (y + (0, 1, YN - 1, 2)[b]) % YN
        for side in range(XN):
            columns = pl.ds(pl.multiple_of(side * (YN * RUN) + sender * RUN, RUN), RUN)
            out_ref[:, columns] = mixed[side].astype(BF16)

    project(0)
    up_b.wait_recv()
    project(1)
    add_core(0)
    down_b.wait_recv()
    project(2)
    add_core(1)
    add_core(2)
    up_far.wait_recv()
    down_far.wait_recv()
    project(3)
    finish(0)
    add_core(3)
    finish(1)
    finish(2)
    finish(3)

    @pl.loop(1, ZN)
    def _(o):
        z_copy(o).wait_send()
        back_copy(o).wait_send()

    @pl.loop(1, ROWS)
    def _(o):
        row_copy(o).wait_send()

    for copy in started:
        copy.wait_send()


def shards(query_in, key_in, value_in, short_filter, decay_rate, residue, out_weight):
    def sems(count):
        return pltpu.SemaphoreType.DMA((2, count))

    return pl.pallas_call(
        kernel,
        out_shape=jax.ShapeDtypeStruct((QTR, 4096), BF16),
        in_specs=[pl.BlockSpec(memory_space=pl.ANY)] * 7,
        out_specs=pl.BlockSpec(memory_space=pltpu.VMEM),
        scratch_shapes=[
            pltpu.VMEM((TOK, CHN), BF16),
            pltpu.VMEM((TOK, CHN), BF16),
            pltpu.VMEM((TOK, CHN), BF16),
            pltpu.VMEM((3, TAPS, CHN), F32),
            pltpu.VMEM((MODES, CHN), F32),
            pltpu.VMEM((MODES, CHN), F32),
            pltpu.VMEM((COLS, CHN), BF16),
            pltpu.VMEM((TILES, 16, 128), F32),
            pltpu.VMEM((TILES, MODES, 128), F32),
            pltpu.VMEM((TILES, MODES, 128), F32),
            pltpu.VMEM((TILES, MODES, 128), F32),
            pltpu.VMEM((TILES, 128), F32),
            pltpu.VMEM((3, TILES, 8 + TOK, 128), F32),
            pltpu.VMEM((8, CHN), F32),
            pltpu.VMEM((8, CHN), F32),
            pltpu.VMEM((TILES, STEPS, SEG, 128), F32),
            pltpu.VMEM((TILES, STEPS, SEG, 128), F32),
            pltpu.VMEM((TILES, MODES, SEG, 128), F32),
            pltpu.VMEM((TILES, MODES, SEG, 128), F32),
            pltpu.VMEM((TILES, MODES, 128), F32),
            pltpu.VMEM((MODES, TILES, 128), F32),
            pltpu.VMEM((ZN, TILES, 128), F32),
            pltpu.VMEM((ZN, TILES, 128), F32),
            pltpu.VMEM((ROWS, TILES, 128), F32),
            pltpu.VMEM((ZN, TILES, 128), F32),
            pltpu.VMEM((MODES, TILES, 128), F32),
            pltpu.VMEM((TILES, TOK, 128), F32),
            pltpu.VMEM((YN, 2, TOK, CHN // 2), BF16),
            pltpu.VMEM((XN, ZN, COLS, CHN), BF16),
            pltpu.VMEM((YN, 2, 2, XN, QTR, RUN), F32),
            pltpu.VMEM((YN, 2, 2, XN, QTR, RUN), BF16),
            pltpu.VMEM((YN, 2, XN, QTR, RUN), BF16),
            pltpu.VMEM((YN, 2, XN, QTR, RUN), BF16),
            pltpu.VMEM((YN, 2, XN, QTR, RUN), BF16),
            pltpu.SemaphoreType.DMA((7,)),
            sems(1),
            sems(ZN),
            sems(ROWS),
            sems(ZN),
            sems(2 * HALF * 3),
            sems(1),
            sems(ZN),
            sems(6),
            sems(YN),
            sems(YN * 2),
        ],
        compiler_params=pltpu.CompilerParams(
            collective_id=0, has_side_effects=True, vmem_limit_bytes=56 * 1024 * 1024
        ),
        cost_estimate=pl.CostEstimate(
            flops=2 * 4 * TOK * CHN * CHN, bytes_accessed=4 * 1024 * 1024, transcendentals=0
        ),
    )(
        query_in, key_in, value_in, short_filter,
        jnp.transpose(decay_rate), jnp.transpose(residue), jnp.transpose(out_weight),
    )


def solution(mesh):
    return jax.shard_map(
        shards,
        mesh=mesh,
        in_specs=(
            P("ctx", "ch"),
            P("ctx", "ch"),
            P("ctx", "ch"),
            P(None, None, "ch"),
            P("ch", None),
            P("ch", None),
            P("ch", "ctx"),
        ),
        out_specs=P(("ctx", "ch"), None),
        check_vma=False,
    )
```

time: 85 us -> 73.2 us (0.86)
  Pallas kernels: 81.2 us -> 71.4 us
  other arithmetic: 0.97 us -> 0 us
    pallas_call x1, Pallas kernels: 81.2 us -> 71.4 us  [shards(): pl.pallas_call(kernel, out_shape=jax.ShapeDtypeStruct((QTR, 4096), BF16),...]
    unnamed x1 -> x0, other arithmetic: 0.97 us -> none
    reshape x3 -> x0, local copies, waits for them, and re-layouts: 0.88 us -> none  [the longest x2 0.87 us: shards(): taps = jnp.transpose(short_filter.reshape(3 * TAPS, TILES, 128), (1, 0, 2))]
where the time goes in v2:
time: 73.2 us; the launch traced here: 73.1 us
  Pallas kernels  71.4 us (98%)
  local copies, waits for them, and re-layouts  1.67 us (2%)
    pallas_call x1, Pallas kernels, shards(): pl.pallas_call(kernel, out_shape=jax.ShapeDtypeStruct((QTR, 4096), BF16),...  71.4 us
    unnamed x1, local copies, waits for them, and re-layouts  1.67 us

profile of v2, /device:TPU:1, one launch (start us, length us, event | category | flops | bytes accessed | tf_op | source)
XLA Modules:
  0.0 73.1 jit_solution(991612654495066226)
XLA Ops:
  0.0 71.4 %shard_map.73 = bf16[32,4096]{1,0:T(8,128)(2,1)} custom-call(bf16[128,1024]{1,0:T(8,128)(2,1)} %q_hbm.1, bf16[128,1024]{1,0:T(8,128)(2,1)} %k_hbm.1, bf16[128,1024]{1,0:T(8,128)(2,1)} %v_hbm.1, f32[3,3,1024]{2,1,0:T(4,128)} %taps_hbm.1, f32[16,1024]{1,0:T(8,128)} %bitcast.3, f32[16,1024]{1,0:T(8,128)} %bitcast.4, bf16[32,1024]{1,0:T(8,128)(2,1)} %bitcast.5), custom_call_target="tpu_custom_call" | custom-call | flops 1073741824 | bytes 4194304 | tf_op jit(solution)/shard_map/pallas_call | solution.py:444
  71.4 1.7 %copy.9 = bf16[32,4096]{1,0:T(8,128)(2,1)} copy(bf16[32,4096]{1,0:T(8,128)(2,1)} %shard_map.73) | data formatting | bytes 524288

commit v3 on v2

--- a/solution.py
+++ b/solution.py
@@ -22,6 +22,7 @@
 RUN = ZN * COLS
 QTR = TOK // 4
 HALF = ZN // 2
+NEAR = ZN // 4
 LENGTH = TOK * XN * YN * ZN
 
 
@@ -42,8 +43,8 @@
     q_in, k_in, v_in, taps_in, rate_in, residue_in, wt_in,
     taps, rates, keeps, weights, line_rate,
     xs, halo_out, halo_in, prod, qconv, local, powers, ends_own, ends, z_in, before, totals, carry_out, carry_in,
-    gate, pooled, wg, part, part_out, part_in, last_out, last_in,
-    load_sem, halo_sem, z_sem, row_sem, back_sem, ring_sem, cross_sem, fore_sem, pool_sem, core_sem, last_sem,
+    gate, pooled, wg, first, part, part_out, part_in, last_out, last_in,
+    load_sem, line_sem, halo_sem, z_sem, row_sem, back_sem, ring_sem, fore_sem, pool_sem, core_sem, last_sem,
 ):
     ctx = lax.axis_index("ctx")
     ch = lax.axis_index("ch")
@@ -88,10 +89,9 @@
     def greet(device):
         pl.semaphore_signal(barrier, inc=1, device_id=device, device_id_type=MESH)
 
-    @pl.loop(1, ZN)
-    def _(o):
-        greet((row * ZN + (z + o) % ZN, ch))
-
+    for o in range(1, NEAR + 1):
+        greet(at(xl, y, (z + o) % ZN))
+        greet(at(xl, y, (z + ZN - o) % ZN))
     for device in (nxt, prv, mate):
         greet(device)
     for b in range(YN):
@@ -110,7 +110,10 @@
         halo_out[2 * s : 2 * s + 2, :] = stream[TOK - 16 :, :].astype(F32)[14:16]
     loads[3].wait()
     wg[xl, z] = wt_in[...]
-    pl.semaphore_wait(barrier, 3 + YN + (ZN - 1) + (ROWS - 1))
+    pl.semaphore_wait(barrier, 3 + YN + 2 * NEAR + (ROWS - 1))
+
+    for o in (NEAR, ZN - NEAR):
+        pl.semaphore_signal(line_sem, inc=1, device_id=at(xl, y, (z + o) % ZN), device_id_type=MESH)
 
     started = []
 
@@ -122,48 +125,54 @@
     halo = go(send(halo_out, halo_in, halo_sem, 0, nxt))
 
     lower, upper = pl.ds(0, COLS // 2), pl.ds(COLS // 2, COLS // 2)
-    chunks = ((xl, upper), (xl, lower), (1 - xl, upper))
     ups, downs, fore = {}, {}, {}
 
-    def piece(side, rows, index):
-        return wg.at[side, lax.rem(index + 2 * ZN, ZN), rows]
-
-    def pass_on(step, c):
-        side, rows = chunks[c]
-        if step < HALF - 1 or (step == HALF - 1 and c < 2):
-            b = piece(side, rows, z - step)
-            ups[step, c] = go(send(b, b, ring_sem, step * 3 + c, z_up))
-        if step < HALF - 1 or (step == HALF - 1 and c == 2):
-            b = piece(side, rows, z + step)
-            downs[step, c] = go(send(b, b, ring_sem, (HALF + step) * 3 + c, z_down))
+    def block(index, rows=None):
+        ref = wg.at[xl, lax.rem(index + 2 * ZN, ZN)]
+        return ref if rows is None else ref.at[rows]
 
     def forward(name, index):
-        b = piece(xl, lower, index)
-        fore[name] = go(send(b, b, fore_sem, name, x_mate))
-
-    b = piece(xl, upper, z)
-    cross = go(send(b, b, cross_sem, 0, x_mate))
-    pass_on(0, 0)
-    pass_on(0, 1)
+        fore[name] = go(send(block(index), block(index), fore_sem, name, x_mate))
+
+    def pass_on(reach, c, hops):
+        rows = (lower, upper)[c]
+        if reach < HALF or c == 0:
+            b = block(z - reach + hops, rows)
+            ups[reach, c] = go(
+                send(b, b, ring_sem, reach * 2 + c, at(xl, y, (z + hops) % ZN))
+            )
+        if reach < HALF or c == 1:
+            b = block(z + reach - hops, rows)
+            downs[reach, c] = go(
+                send(b, b, ring_sem, (HALF + 1 + reach) * 2 + c, at(xl, y, (z + ZN - hops) % ZN))
+            )
+
+    for c in range(2):
+        pass_on(2, c, 2)
+    for c in range(2):
+        pass_on(1, c, 1)
     forward(0, z)
 
+    def arrived(reach, c):
+        if (reach, c) in ups:
+            ups[reach, c].wait_recv()
+        if (reach, c) in downs:
+            downs[reach, c].wait_recv()
+
     def tick(step):
-        for c in range(3):
-            if step == 0:
-                if c == 2:
-                    cross.wait_recv()
-                    pass_on(0, 2)
-                continue
-            if (step - 1, c) in ups:
-                ups[step - 1, c].wait_recv()
-            if (step - 1, c) in downs:
-                downs[step - 1, c].wait_recv()
-            if step < HALF:
-                pass_on(step, c)
-            if c == 1:
-                forward(step, z - step)
-                if step < HALF:
-                    forward(HALF + step, z + step)
+        reach = step + 1
+        for c in range(2):
+            if reach == 2:
+                arrived(1, c)
+            arrived(reach, c)
+            if reach < HALF:
+                pass_on(reach + 1, c, 1)
+        if reach == 2:
+            forward(1, z - 1)
+            forward(HALF + 1, z + 1)
+        forward(reach, z - reach)
+        if reach < HALF:
+            forward(HALF + reach, z + reach)
 
     loads[4].wait()
     loads[5].wait()
@@ -209,8 +218,6 @@
     def _(j):
         features(j, 0, STEPS)
 
-    tick(0)
-
     @pl.loop(0, TILES)
     def _(j):
         rate = rates[j]
@@ -248,9 +255,12 @@
         for n in range(MODES):
             ends[n, pl.ds(j, 1), :] = total[n : n + 1]
 
-    def z_copy(o):
+    def z_copy(i):
+        o = HALF + (i // 2) * (1 - 2 * (i % 2))
         to = (z + o) % ZN
         return send(ends.at[to], z_in.at[z], z_sem, o, (row * ZN + to, ch))
+
+    pl.semaphore_wait(line_sem, 2)
 
     @pl.loop(1, ZN)
     def _(o):
@@ -291,6 +301,7 @@
         row_copy(o).start()
 
     tick(3)
+    tick(4)
 
     @pl.loop(1, ROWS)
     def _(o):
@@ -304,7 +315,8 @@
         carry_out[zz] = before[zz] + state
         state = keep * state
 
-    def back_copy(o):
+    def back_copy(i):
+        o = HALF + (i // 2) * (1 - 2 * (i % 2))
         to = (z + o) % ZN
         return send(carry_out.at[to], carry_in.at[z], back_sem, o, (row * ZN + to, ch))
 
@@ -313,8 +325,8 @@
         back_copy(o).start()
 
     carry_in[z] = carry_out[z]
-    tick(4)
     tick(5)
+    tick(6)
 
     @pl.loop(1, ZN)
     def _(o):
@@ -352,35 +364,36 @@
     up_b = pool(0, 1, 1, 2, y_up)
     down_b = pool(0, 2, 0, 3, y_down)
 
-    tick(6)
     tick(7)
     up_a.wait_recv()
     up_far = pool(1, 3, 0, 4, y_up)
     down_a.wait_recv()
     down_far = pool(2, 3, 1, 5, y_down)
-    tick(8)
     for copy in fore.values():
         copy.wait_recv()
 
     to_core, to_owner = {}, {}
 
-    def project(b):
+    def product(b, half, side):
+        depth = slice(half * (CHN // 2), (half + 1) * (CHN // 2))
+        return lax.dot_general(
+            pooled[b, half],
+            wg[side, :, :, depth].reshape(RUN, CHN // 2),
+            (((1,), (1,)), ((), ())),
+            preferred_element_type=F32,
+        )
+
+    def project(b, sums):
         for side in range(XN):
-            sums = 0.0
-            for half in range(2):
-                depth = slice(half * (CHN // 2), (half + 1) * (CHN // 2))
-                sums = sums + lax.dot_general(
-                    pooled[b, half],
-                    wg[side, :, :, depth].reshape(RUN, CHN // 2),
-                    (((1,), (1,)), ((), ())),
-                    preferred_element_type=F32,
-                )
             for h in range(2):
                 for c in range(2):
-                    quarter = sums[(h * 2 + c) * QTR : (h * 2 + c + 1) * QTR]
+                    quarter = sums[side][(h * 2 + c) * QTR : (h * 2 + c + 1) * QTR]
                     part[b, c, h, side] = quarter
                     part_out[b, c, h, side] = quarter.astype(BF16)
         to_core[b] = go(send(part_out.at[b, 1 - core], part_in.at[b], core_sem, b, mate))
+
+    def both(b):
+        return [product(b, 0, side) + product(b, 1, side) for side in range(XN)]
 
     def add_core(b):
         to_core[b].wait_recv()
@@ -407,17 +420,19 @@
             columns = pl.ds(pl.multiple_of(side * (YN * RUN) + sender * RUN, RUN), RUN)
             out_ref[:, columns] = mixed[side].astype(BF16)
 
-    project(0)
+    project(0, both(0))
     up_b.wait_recv()
-    project(1)
+    project(1, both(1))
     add_core(0)
     down_b.wait_recv()
-    project(2)
+    project(2, both(2))
     add_core(1)
+    up_far.wait_recv()
+    for side in range(XN):
+        first[side] = product(3, 0, side)
     add_core(2)
-    up_far.wait_recv()
     down_far.wait_recv()
-    project(3)
+    project(3, [first[side] + product(3, 1, side) for side in range(XN)])
     finish(0)
     add_core(3)
     finish(1)
@@ -476,18 +491,19 @@
             pltpu.VMEM((TILES, TOK, 128), F32),
             pltpu.VMEM((YN, 2, TOK, CHN // 2), BF16),
             pltpu.VMEM((XN, ZN, COLS, CHN), BF16),
+            pltpu.VMEM((XN, TOK, RUN), F32),
             pltpu.VMEM((YN, 2, 2, XN, QTR, RUN), F32),
             pltpu.VMEM((YN, 2, 2, XN, QTR, RUN), BF16),
             pltpu.VMEM((YN, 2, XN, QTR, RUN), BF16),
             pltpu.VMEM((YN, 2, XN, QTR, RUN), BF16),
             pltpu.VMEM((YN, 2, XN, QTR, RUN), BF16),
             pltpu.SemaphoreType.DMA((7,)),
+            pltpu.SemaphoreType.REGULAR,
             sems(1),
             sems(ZN),
             sems(ROWS),
             sems(ZN),
-            sems(2 * HALF * 3),
-            sems(1),
+            sems(2 * (HALF + 1) * 2),
             sems(ZN),
             sems(6),
             sems(YN),

time: 73.2 us -> 67.8 us (0.926)
  Pallas kernels: 71.4 us -> 65.9 us
    pallas_call x1, Pallas kernels: 71.4 us -> 65.9 us  [shards(): pl.pallas_call(kernel, out_shape=jax.ShapeDtypeStruct((QTR, 4096), BF16),...]
where the time goes in v3:
time: 67.8 us; the launch traced here: 67.6 us
  Pallas kernels  65.9 us (97%)
  local copies, waits for them, and re-layouts  1.67 us (2%)
    pallas_call x1, Pallas kernels, shards(): pl.pallas_call(kernel, out_shape=jax.ShapeDtypeStruct((QTR, 4096), BF16),...  65.9 us
    unnamed x1, local copies, waits for them, and re-layouts  1.67 us

profile of v3, /device:TPU:1, one launch (start us, length us, event | category | flops | bytes accessed | tf_op | source)
XLA Modules:
  0.0 67.6 jit_solution(16835831836246555513)
XLA Ops:
  0.0 65.9 %shard_map.73 = bf16[32,4096]{1,0:T(8,128)(2,1)} custom-call(bf16[128,1024]{1,0:T(8,128)(2,1)} %q_hbm.1, bf16[128,1024]{1,0:T(8,128)(2,1)} %k_hbm.1, bf16[128,1024]{1,0:T(8,128)(2,1)} %v_hbm.1, f32[3,3,1024]{2,1,0:T(4,128)} %taps_hbm.1, f32[16,1024]{1,0:T(8,128)} %bitcast.3, f32[16,1024]{1,0:T(8,128)} %bitcast.4, bf16[32,1024]{1,0:T(8,128)(2,1)} %bitcast.5), custom_call_target="tpu_custom_call" | custom-call | flops 1073741824 | bytes 4194304 | tf_op jit(solution)/shard_map/pallas_call | solution.py:459
  65.9 1.7 %copy.9 = bf16[32,4096]{1,0:T(8,128)(2,1)} copy(bf16[32,4096]{1,0:T(8,128)(2,1)} %shard_map.73) | data formatting | bytes 524288

commit v4 on v3

--- a/solution.py
+++ b/solution.py
@@ -20,8 +20,11 @@
 STEPS = TOK // SEG
 COLS = 32
 RUN = ZN * COLS
+SPAN = RUN // 2
 QTR = TOK // 4
 HALF = ZN // 2
+RING = ZN // 2
+REACH = RING // 2
 NEAR = ZN // 4
 LENGTH = TOK * XN * YN * ZN
 
@@ -43,8 +46,8 @@
     q_in, k_in, v_in, taps_in, rate_in, residue_in, wt_in,
     taps, rates, keeps, weights, line_rate,
     xs, halo_out, halo_in, prod, qconv, local, powers, ends_own, ends, z_in, before, totals, carry_out, carry_in,
-    gate, pooled, wg, first, part, part_out, part_in, last_out, last_in,
-    load_sem, line_sem, halo_sem, z_sem, row_sem, back_sem, ring_sem, fore_sem, pool_sem, core_sem, last_sem,
+    gate, pooled, wg, first, part, part_out, part_in, last_out, last_in, woven, turns,
+    load_sem, line_sem, halo_sem, z_sem, row_sem, back_sem, ring_sem, twin_sem, fore_sem, pool_sem, core_sem, last_sem,
 ):
     ctx = lax.axis_index("ctx")
     ch = lax.axis_index("ch")
@@ -79,10 +82,12 @@
     prv = ((ctx + XN * YN * ZN - 1) % (XN * YN * ZN), ch)
     mate = (ctx, hi * 2 + 1 - core)
     far_ch = (1 - hi) * 2 + core
-    z_up, z_down = at(xl, y, (z + 1) % ZN), at(xl, y, (z + ZN - 1) % ZN)
-    y_of = (y, (y + YN - 1) % YN, (y + 1) % YN, (y + 2) % YN)
-    y_down, y_up = at(xl, y_of[1], z), at(xl, y_of[2], z)
     x_mate = at(1 - xl, y, z)
+
+    y_of = (y, y + 1 - 2 * (y % 2), y, y + 1 - 2 * (y % 2))
+    z_of = (z, z, z + 1 - 2 * (z % 2), z + 1 - 2 * (z % 2))
+    y_mate, z_mate = at(xl, y_of[1], z), at(xl, y, z_of[2])
+    y_twin = at(xl, YN - 1 - y, z)
 
     barrier = pltpu.get_barrier_semaphore()
 
@@ -94,8 +99,9 @@
         greet(at(xl, y, (z + ZN - o) % ZN))
     for device in (nxt, prv, mate):
         greet(device)
-    for b in range(YN):
-        greet(at(xl, y_of[b], z, far_ch))
+    for b in range(4):
+        greet(at(xl, y_of[b], z_of[b], far_ch))
+    greet(at(xl, y_of[3], z_of[3]))
 
     @pl.loop(1, ROWS)
     def _(o):
@@ -109,8 +115,8 @@
     for s, stream in enumerate(streams):
         halo_out[2 * s : 2 * s + 2, :] = stream[TOK - 16 :, :].astype(F32)[14:16]
     loads[3].wait()
-    wg[xl, z] = wt_in[...]
-    pl.semaphore_wait(barrier, 3 + YN + 2 * NEAR + (ROWS - 1))
+    wg[xl * 2 + y // 2, z // 2] = wt_in[...]
+    pl.semaphore_wait(barrier, 3 + 5 + 2 * NEAR + (ROWS - 1))
 
     for o in (NEAR, ZN - NEAR):
         pl.semaphore_signal(line_sem, inc=1, device_id=at(xl, y, (z + o) % ZN), device_id_type=MESH)
@@ -125,54 +131,63 @@
     halo = go(send(halo_out, halo_in, halo_sem, 0, nxt))
 
     lower, upper = pl.ds(0, COLS // 2), pl.ds(COLS // 2, COLS // 2)
-    ups, downs, fore = {}, {}, {}
-
-    def block(index, rows=None):
-        ref = wg.at[xl, lax.rem(index + 2 * ZN, ZN)]
+    ups, downs, twin, fore = {}, {}, {}, {}
+    place = xl * 2 + y // 2
+    beside = xl * 2 + 1 - y // 2
+
+    def block(where, index, rows=None):
+        ref = wg.at[where, lax.rem(index + 2 * RING, RING)]
         return ref if rows is None else ref.at[rows]
 
     def forward(name, index):
-        fore[name] = go(send(block(index), block(index), fore_sem, name, x_mate))
-
-    def pass_on(reach, c, hops):
+        b = block(place, index)
+        twin[name] = go(send(b, b, twin_sem, name, y_twin))
+        fore[name] = go(send(b, b, fore_sem, name, x_mate))
+
+    def forward_beside(name, index):
+        twin[name].wait_recv()
+        b = block(beside, index)
+        fore[RING + name] = go(send(b, b, fore_sem, RING + name, x_mate))
+
+    def pass_on(reach, c):
         rows = (lower, upper)[c]
-        if reach < HALF or c == 0:
-            b = block(z - reach + hops, rows)
-            ups[reach, c] = go(
-                send(b, b, ring_sem, reach * 2 + c, at(xl, y, (z + hops) % ZN))
+        if reach < REACH or c == 0:
+            b = block(place, z // 2 - reach + 1, rows)
+            ups[reach, c] = go(send(b, b, ring_sem, reach * 2 + c, at(xl, y, (z + 2) % ZN)))
+        if reach < REACH or c == 1:
+            b = block(place, z // 2 + reach - 1, rows)
+            downs[reach, c] = go(
+                send(b, b, ring_sem, (REACH + 1 + reach) * 2 + c, at(xl, y, (z + ZN - 2) % ZN))
             )
-        if reach < HALF or c == 1:
-            b = block(z + reach - hops, rows)
-            downs[reach, c] = go(
-                send(b, b, ring_sem, (HALF + 1 + reach) * 2 + c, at(xl, y, (z + ZN - hops) % ZN))
-            )
 
     for c in range(2):
-        pass_on(2, c, 2)
-    for c in range(2):
-        pass_on(1, c, 1)
-    forward(0, z)
-
-    def arrived(reach, c):
-        if (reach, c) in ups:
-            ups[reach, c].wait_recv()
-        if (reach, c) in downs:
-            downs[reach, c].wait_recv()
-
-    def tick(step):
-        reach = step + 1
+        pass_on(1, c)
+    forward(0, z // 2)
+
+    def names(reach):
+        if reach == 0:
+            return [(0, 0)]
+        return [(reach, -reach)] + ([(REACH + reach, reach)] if reach < REACH else [])
+
+    def tick(reach):
         for c in range(2):
-            if reach == 2:
-                arrived(1, c)
-            arrived(reach, c)
-            if reach < HALF:
-                pass_on(reach + 1, c, 1)
-        if reach == 2:
-            forward(1, z - 1)
-            forward(HALF + 1, z + 1)
-        forward(reach, z - reach)
-        if reach < HALF:
-            forward(HALF + reach, z + reach)
+            if (reach, c) in ups:
+                ups[reach, c].wait_recv()
+            if (reach, c) in downs:
+                downs[reach, c].wait_recv()
+            if reach < REACH:
+                pass_on(reach + 1, c)
+        if reach <= REACH:
+            for name, away in names(reach):
+                forward(name, z // 2 + away)
+        for name, away in names(reach - 1):
+            forward_beside(name, z // 2 + away)
+
+    source = lax.broadcasted_iota(jnp.int32, (RUN, RUN), 0)
+    target = lax.broadcasted_iota(jnp.int32, (RUN, RUN), 1)
+    parity = (source // SPAN + z) % 2
+    wanted = (source % SPAN) // COLS * (2 * COLS) + parity * COLS + source % COLS
+    turns[...] = jnp.where(wanted == target, 1.0, 0.0).astype(BF16)
 
     loads[4].wait()
     loads[5].wait()
@@ -267,7 +282,6 @@
         z_copy(o).start()
 
     z_in[z] = ends[z]
-    tick(1)
 
     @pl.loop(0, TILES)
     def _(j):
@@ -278,11 +292,12 @@
             powers[j, n] = power
             local[j, n] = local[j, n] + jnp.where(later, power * extra[n : n + 1], 0.0)
 
-    tick(2)
+    tick(1)
 
     @pl.loop(1, ZN)
     def _(o):
         z_copy(o).wait_recv()
+
 
     rate = line_rate[...]
     keep = jnp.exp(rate * -float(TOK))
@@ -300,12 +315,13 @@
     def _(o):
         row_copy(o).start()
 
-    tick(3)
-    tick(4)
+
+    tick(2)
 
     @pl.loop(1, ROWS)
     def _(o):
         row_copy(o).wait_recv()
+
 
     keep_row = jnp.exp(rate * -float(TOK * ZN))
     state = jnp.zeros((SEG, 128), F32)
@@ -325,12 +341,14 @@
         back_copy(o).start()
 
     carry_in[z] = carry_out[z]
-    tick(5)
-    tick(6)
+
+    tick(3)
+    tick(4)
 
     @pl.loop(1, ZN)
     def _(o):
         back_copy(o).wait_recv()
+
 
     def gated(half):
         @pl.loop(half * (TILES // 2), (half + 1) * (TILES // 2))
@@ -352,52 +370,52 @@
 
         for i in range(TILES // 2):
             lanes = slice(i * 128, (i + 1) * 128)
-            pooled[0, half, :, lanes] = gate[half * (TILES // 2) + i].astype(BF16)
+            pooled[half, 0, :, lanes] = gate[half * (TILES // 2) + i].astype(BF16)
 
     def pool(slot, to_slot, half, index, device):
-        return go(send(pooled.at[slot, half], pooled.at[to_slot, half], pool_sem, index, device))
+        return go(send(pooled.at[half, slot], pooled.at[half, to_slot], pool_sem, index, device))
 
     gated(0)
-    up_a = pool(0, 1, 0, 0, y_up)
+    z_a = pool(0, 2, 0, 0, z_mate)
     gated(1)
-    down_a = pool(0, 2, 1, 1, y_down)
-    up_b = pool(0, 1, 1, 2, y_up)
-    down_b = pool(0, 2, 0, 3, y_down)
-
-    tick(7)
-    up_a.wait_recv()
-    up_far = pool(1, 3, 0, 4, y_up)
-    down_a.wait_recv()
-    down_far = pool(2, 3, 1, 5, y_down)
-    for copy in fore.values():
-        copy.wait_recv()
+    y_a = pool(0, 1, 1, 1, y_mate)
+    z_b = pool(0, 2, 1, 2, z_mate)
+    y_b = pool(0, 1, 0, 3, y_mate)
+
+    tick(5)
 
     to_core, to_owner = {}, {}
 
-    def product(b, half, side):
+    def product(first_b, last_b, half, side):
         depth = slice(half * (CHN // 2), (half + 1) * (CHN // 2))
         return lax.dot_general(
-            pooled[b, half],
-            wg[side, :, :, depth].reshape(RUN, CHN // 2),
+            pooled[half, first_b : last_b + 1].reshape((last_b + 1 - first_b) * TOK, CHN // 2),
+            wg[2 * side : 2 * side + 2, :, :, depth].reshape(RUN, CHN // 2),
             (((1,), (1,)), ((), ())),
             preferred_element_type=F32,
         )
 
-    def project(b, sums):
+    def project(b, side, sums):
+        for h in range(2):
+            for c in range(2):
+                quarter = sums[(h * 2 + c) * QTR : (h * 2 + c + 1) * QTR]
+                part[b, c, h, side] = quarter
+                part_out[b, c, h, side] = quarter.astype(BF16)
+
+    def whole(first_b, last_b):
         for side in range(XN):
-            for h in range(2):
-                for c in range(2):
-                    quarter = sums[side][(h * 2 + c) * QTR : (h * 2 + c + 1) * QTR]
-                    part[b, c, h, side] = quarter
-                    part_out[b, c, h, side] = quarter.astype(BF16)
+            sums = product(first_b, last_b, 0, side) + product(first_b, last_b, 1, side)
+            for b in range(first_b, last_b + 1):
+                project(b, side, sums[(b - first_b) * TOK : (b + 1 - first_b) * TOK])
+        for b in range(first_b, last_b + 1):
+            exchange(b)
+
+    def exchange(b):
         to_core[b] = go(send(part_out.at[b, 1 - core], part_in.at[b], core_sem, b, mate))
-
-    def both(b):
-        return [product(b, 0, side) + product(b, 1, side) for side in range(XN)]
 
     def add_core(b):
         to_core[b].wait_recv()
-        for same, h in ((0, hi), (1, 1 - hi)):
+        for same, h in ((1, 1 - hi), (0, hi)):
             sums = part[b, core, h] + part_in[b, h].astype(F32)
             last_out[b, same] = sums.astype(BF16)
             if b == 0 and same == 0:
@@ -406,38 +424,53 @@
                 to_owner[b, same] = go(
                     send(
                         last_out.at[b, same], last_in.at[b, same], last_sem, b * 2 + same,
-                        at(xl, y_of[b], z, h * 2 + core),
+                        at(xl, y_of[b], z_of[b], h * 2 + core),
                     )
                 )
 
-    def finish(b):
-        for same in range(2):
-            if (b, same) in to_owner:
-                to_owner[b, same].wait_recv()
-        mixed = last_in[b, 0].astype(F32) + last_in[b, 1].astype(F32)
-        sender = (y + (0, 1, YN - 1, 2)[b]) % YN
+    def finish(bs):
+        for i, b in enumerate(bs):
+            for same in range(2):
+                if (b, same) in to_owner:
+                    to_owner[b, same].wait_recv()
+            mixed = (last_in[b, 0].astype(F32) + last_in[b, 1].astype(F32)).astype(BF16)
+            for side in range(XN):
+                for k in range(2):
+                    woven[side * 2 + k, :, i * SPAN : (i + 1) * SPAN] = mixed[side, :, k * SPAN : (k + 1) * SPAN]
+        spread = lax.dot_general(
+            woven[...].reshape(4 * QTR, RUN), turns[...], (((1,), (0,)), ((), ())),
+            preferred_element_type=F32,
+        ).astype(BF16)
+        sender = y_of[bs[0]]
+        role = (sender + sender // 2) % 2
         for side in range(XN):
-            columns = pl.ds(pl.multiple_of(side * (YN * RUN) + sender * RUN, RUN), RUN)
-            out_ref[:, columns] = mixed[side].astype(BF16)
-
-    project(0, both(0))
-    up_b.wait_recv()
-    project(1, both(1))
+            for k, at_y in enumerate((role, YN - 1 - role)):
+                columns = pl.ds(pl.multiple_of(side * (YN * RUN) + at_y * RUN, RUN), RUN)
+                out_ref[:, columns] = spread[(side * 2 + k) * QTR : (side * 2 + k + 1) * QTR]
+
+    z_a.wait_recv()
+    far_a = pool(2, 3, 0, 4, y_mate)
+    y_a.wait_recv()
+    far_b = pool(1, 3, 1, 5, z_mate)
+    for copy in fore.values():
+        copy.wait_recv()
+    whole(0, 0)
+    y_b.wait_recv()
+    z_b.wait_recv()
+    whole(1, 2)
     add_core(0)
-    down_b.wait_recv()
-    project(2, both(2))
+    far_a.wait_recv()
+    for side in range(XN):
+        first[side] = product(3, 3, 0, side)
     add_core(1)
-    up_far.wait_recv()
+    add_core(2)
+    far_b.wait_recv()
     for side in range(XN):
-        first[side] = product(3, 0, side)
-    add_core(2)
-    down_far.wait_recv()
-    project(3, [first[side] + product(3, 1, side) for side in range(XN)])
-    finish(0)
+        project(3, side, first[side] + product(3, 3, 1, side))
+    exchange(3)
+    finish((0, 2))
     add_core(3)
-    finish(1)
-    finish(2)
-    finish(3)
+    finish((1, 3))
 
     @pl.loop(1, ZN)
     def _(o):
@@ -489,21 +522,24 @@
             pltpu.VMEM((ZN, TILES, 128), F32),
             pltpu.VMEM((MODES, TILES, 128), F32),
             pltpu.VMEM((TILES, TOK, 128), F32),
-            pltpu.VMEM((YN, 2, TOK, CHN // 2), BF16),
-            pltpu.VMEM((XN, ZN, COLS, CHN), BF16),
+            pltpu.VMEM((2, 4, TOK, CHN // 2), BF16),
+            pltpu.VMEM((2 * XN, RING, COLS, CHN), BF16),
             pltpu.VMEM((XN, TOK, RUN), F32),
             pltpu.VMEM((YN, 2, 2, XN, QTR, RUN), F32),
             pltpu.VMEM((YN, 2, 2, XN, QTR, RUN), BF16),
             pltpu.VMEM((YN, 2, XN, QTR, RUN), BF16),
             pltpu.VMEM((YN, 2, XN, QTR, RUN), BF16),
             pltpu.VMEM((YN, 2, XN, QTR, RUN), BF16),
+            pltpu.VMEM((4, QTR, RUN), BF16),
+            pltpu.VMEM((RUN, RUN), BF16),
             pltpu.SemaphoreType.DMA((7,)),
             pltpu.SemaphoreType.REGULAR,
             sems(1),
             sems(ZN),
             sems(ROWS),
             sems(ZN),
-            sems(2 * (HALF + 1) * 2),
+            sems(2 * (REACH + 1) * 2),
+            sems(RING),
             sems(ZN),
             sems(6),
             sems(YN),

time: 67.8 us -> 62.8 us (0.926)
  the two profiles are of different devices: /device:TPU:1 before, /device:TPU:8 now
where the time goes in v4:
time: 62.8 us; the launch traced here: 62.6 us
  Pallas kernels  61 us (97%)
  local copies, waits for them, and re-layouts  1.67 us (3%)
    pallas_call x1, Pallas kernels, shards(): pl.pallas_call(kernel, out_shape=jax.ShapeDtypeStruct((QTR, 4096), BF16),...  61 us
    unnamed x1, local copies, waits for them, and re-layouts  1.67 us

profile of v4, /device:TPU:8, one launch (start us, length us, event | category | flops | bytes accessed | tf_op | source)
XLA Modules:
  0.0 62.6 jit_solution(716473897635006252)
XLA Ops:
  0.0 61.0 %shard_map.73 = bf16[32,4096]{1,0:T(8,128)(2,1)} custom-call(bf16[128,1024]{1,0:T(8,128)(2,1)} %q_hbm.1, bf16[128,1024]{1,0:T(8,128)(2,1)} %k_hbm.1, bf16[128,1024]{1,0:T(8,128)(2,1)} %v_hbm.1, f32[3,3,1024]{2,1,0:T(4,128)} %taps_hbm.1, f32[16,1024]{1,0:T(8,128)} %bitcast.3, f32[16,1024]{1,0:T(8,128)} %bitcast.4, bf16[32,1024]{1,0:T(8,128)(2,1)} %bitcast.5), custom_call_target="tpu_custom_call" | custom-call | flops 1073741824 | bytes 4194304 | tf_op jit(solution)/shard_map/pallas_call | solution.py:492
  61.0 1.7 %copy.9 = bf16[32,4096]{1,0:T(8,128)(2,1)} copy(bf16[32,4096]{1,0:T(8,128)(2,1)} %shard_map.73) | data formatting | bytes 524288

commit v5 on v4

--- a/solution.py
+++ b/solution.py
@@ -468,8 +468,8 @@
     for side in range(XN):
         project(3, side, first[side] + product(3, 3, 1, side))
     exchange(3)
+    add_core(3)
     finish((0, 2))
-    add_core(3)
     finish((1, 3))
 
     @pl.loop(1, ZN)

time: 62.8 us -> 61.6 us (0.981)
  the two profiles are of different devices: /device:TPU:8 before, /device:TPU:1 now
where the time goes in v5:
time: 61.6 us; the launch traced here: 61.4 us
  Pallas kernels  59.7 us (97%)
  local copies, waits for them, and re-layouts  1.67 us (3%)
    pallas_call x1, Pallas kernels, shards(): pl.pallas_call(kernel, out_shape=jax.ShapeDtypeStruct((QTR, 4096), BF16),...  59.7 us
    unnamed x1, local copies, waits for them, and re-layouts  1.67 us

profile of v5, /device:TPU:1, one launch (start us, length us, event | category | flops | bytes accessed | tf_op | source)
XLA Modules:
  0.0 61.4 jit_solution(12895970144036388735)
XLA Ops:
  0.0 59.7 %shard_map.73 = bf16[32,4096]{1,0:T(8,128)(2,1)} custom-call(bf16[128,1024]{1,0:T(8,128)(2,1)} %q_hbm.1, bf16[128,1024]{1,0:T(8,128)(2,1)} %k_hbm.1, bf16[128,1024]{1,0:T(8,128)(2,1)} %v_hbm.1, f32[3,3,1024]{2,1,0:T(4,128)} %taps_hbm.1, f32[16,1024]{1,0:T(8,128)} %bitcast.3, f32[16,1024]{1,0:T(8,128)} %bitcast.4, bf16[32,1024]{1,0:T(8,128)(2,1)} %bitcast.5), custom_call_target="tpu_custom_call" | custom-call | flops 1073741824 | bytes 4194304 | tf_op jit(solution)/shard_map/pallas_call | solution.py:492
  59.7 1.7 %copy.9 = bf16[32,4096]{1,0:T(8,128)(2,1)} copy(bf16[32,4096]{1,0:T(8,128)(2,1)} %shard_map.73) | data formatting | bytes 524288
